TPU v7x, 32 devices: a whole 2x2x4 slice. The times are simulated.
32 devices in a mesh: groups: 2 (over x), row: 4 (over y, core), col: 4 (over z).
Axes of the slice: x: 2, y: 2, z: 4, core: 2. Of those that a mesh axis runs over, the one named last changes fastest.
Arguments:
- zroot: float32 [4096, 2048], P(('groups', 'row')), parts along dimension 0, as said below
- panel_one: float32 [8, 2048, 1024], P(('groups', 'col'), 'row'), parts along dimension 0, may hold values from -0.125 to 0.125
- inv_one: float32 [8, 1024, 1024], P(('groups', 'col')), parts along dimension 0
- panel_two_j: float32 [16, 1024, 512], P(('groups', 'col'), 'row'), parts along dimension 0, may hold values from -0.109375 to 0.109375
- panel_two_r: float32 [16, 2048, 512], P(('groups', 'col'), 'row'), parts along dimension 0, may hold values from -0.109375 to 0.109375
- inv_two: float32 [16, 512, 512], P(('groups', 'col')), parts along dimension 0
- parents: int32 [16], P(('groups', 'col')), parts along dimension 0, may hold values from 0 to 3
- widths: int32 [16], P(('groups', 'col')), parts along dimension 0, may hold values from 256 to 512, as said below
- pattern_j: int32 [16, 16], P(('groups', 'col'), 'row'), parts along dimension 0, may hold values 0 or 1
- pattern_r: int32 [16, 32], P(('groups', 'col'), 'row'), parts along dimension 0, may hold values 0 or 1
Outputs:
- var_one: float32 [8, 1024], P(('groups', 'col'), 'row'), parts along dimension 0
- var_two: float32 [16, 512], P(('groups', 'col'), 'row'), parts along dimension 0
- z_two_j: float32 [16, 1024, 512], P(('groups', 'col'), 'row'), parts along dimension 0
- z_two_r: float32 [16, 2048, 512], P(('groups', 'col'), 'row'), parts along dimension 0
There are 2 independent parts, one for each index of `groups`. A program takes and returns all parts, laid end to end along the dimension named above; each array names one. Nothing has to cross between parts.
Inputs may be any that keep to these rules, and one draw needn't show every extreme that they name: zroot is symmetric: it equals its transpose up to rounding, as a selected inverse block of a symmetric matrix does. `widths`: the live width of each level-2 supernode; columns at or past it are padding. `parents`: index of the level-1 parent of each level-2 supernode. `pattern_j`: 1 where a tile of 64 rows of the panel is stored. `pattern_r`: 1 where a tile of 64 rows of the panel is stored.
All inputs are finite; a program needn't handle non-finite values. No bound on the sum of `pattern_j` or of `pattern_r` on one device may be relied on, other than what follows from the above.
Results may differ from a plain program's by a relative error of at most 0.0003.
Values sent between devices are 32-bit elements; how exact they have to be, the bound alone decides.
A program may use at most 128 MiB of HBM per device.

v0:
```python
import jax
import jax.numpy as jnp
from jax import lax
from jax.sharding import PartitionSpec as P

TILE = 64
PRECISION = lax.Precision.HIGH


def product(left, right):
    return jnp.dot(left, right, precision=PRECISION, preferred_element_type=jnp.float32)


def crossed(left, right):
    return lax.dot_general(
        left, right, (((0,), (0,)), ((), ())), precision=PRECISION, preferred_element_type=jnp.float32
    )


def swap(block, bit):
    n = lax.axis_size("row")
    return lax.ppermute(block, "row", [(i, i ^ bit) for i in range(n)])


def own_first(array, axis):
    n = lax.axis_size("row")
    me = lax.axis_index("row")
    share = array.shape[axis] // n
    pieces = [
        lax.dynamic_slice_in_dim(array, (me ^ d) * share, share, axis) for d in range(n)
    ]
    return jnp.concatenate(pieces, axis)


def row_blocks(block):
    n = lax.axis_size("row")
    held = {0: block}
    bit = n // 2
    while bit:
        for d in sorted(held):
            held[d | bit] = swap(held[d], bit)
        bit //= 2
    return [held[d] for d in range(n)]


def row_sum(pieces):
    n = lax.axis_size("row")
    held = dict(enumerate(pieces))
    bit = 1
    while bit < n:
        for d in [d for d in sorted(held) if not d & bit]:
            held[d] = held[d] + swap(held.pop(d | bit), bit)
        bit *= 2
    return held[0]


def reordered(block, d):
    n = lax.axis_size("row")
    share = block.shape[1] // n
    return jnp.concatenate(
        [block[:, (d ^ e) * share : ((d ^ e) + 1) * share] for e in range(n)], 1
    )


def body(
    zroot,
    panel_one,
    inv_one,
    panel_two_j,
    panel_two_r,
    inv_two,
    parents,
    widths,
    pattern_j,
    pattern_r,
):
    n = lax.axis_size("row")
    width_one = inv_one.shape[1]
    node_rows = width_one // n
    nodes, width_two = inv_two.shape[:2]
    root_rows = zroot.shape[0]

    inverse = own_first(inv_one[0], 1)
    factor = product(panel_one[0], inverse)
    all_factors = lax.all_gather(factor, "col", axis=0)
    gram = crossed(inverse[:, :node_rows], inverse)
    factor_tied, gram = lax.optimization_barrier((factor, gram))
    all_grams = lax.all_gather(gram, "col", axis=0)

    live = (jnp.arange(width_two)[None, :] < widths[:, None]).astype(jnp.float32)
    mask_j = jnp.repeat(pattern_j.astype(jnp.float32), TILE, axis=1)
    mask_r = jnp.repeat(pattern_r.astype(jnp.float32), TILE, axis=1)
    factor_j = []
    factor_r = []
    for i in range(nodes):
        masked_j = panel_two_j[i] * mask_j[i][:, None] * live[i][None, :]
        masked_r = panel_two_r[i] * mask_r[i][:, None] * live[i][None, :]
        factor_j.append(product(masked_j, inv_two[i]))
        factor_r.append(product(masked_r, inv_two[i]))
    near_j = jnp.concatenate(factor_j, 1)
    full_j = jnp.concatenate(row_blocks(near_j), 0)

    root = own_first(zroot, 1)
    full_factor = jnp.concatenate(
        [reordered(block, d) for d, block in enumerate(row_blocks(factor))], 0
    )
    image = product(root, full_factor)
    terms = jnp.sum(factor * image, axis=0).reshape(n, node_rows)
    own_squares = jnp.sum(inverse[:, :node_rows] ** 2, axis=0)
    var_one = (own_squares + row_sum([terms[d] for d in range(n)]))[None, :]

    all_factors, var_one = lax.optimization_barrier((all_factors, var_one))

    parent_factor = [
        lax.dynamic_index_in_dim(all_factors, parents[i], 0, False) for i in range(nodes)
    ]
    reduced = [
        factor_r[i] - product(parent_factor[i], full_j[:, i * width_two : (i + 1) * width_two])
        for i in range(nodes)
    ]
    block_r = []
    sums_j = []
    for i in range(nodes):
        block_r.append(-product(root, jnp.concatenate(row_blocks(reduced[i]), 0)))
        upper = crossed(parent_factor[i], block_r[i]).reshape(n, node_rows, width_two)
        sums_j.append(row_sum([upper[d] for d in range(n)]))
    block_j = []
    for i in range(nodes):
        parent_gram = lax.dynamic_index_in_dim(all_grams, parents[i], 0, False)
        near = product(parent_gram, full_j[:, i * width_two : (i + 1) * width_two])
        block_j.append(-(near + sums_j[i]))

    corrections = jnp.stack(
        [
            jnp.sum(factor_j[i] * block_j[i], axis=0) + jnp.sum(factor_r[i] * block_r[i], axis=0)
            for i in range(nodes)
        ]
    )
    share = width_two // n
    me = lax.axis_index("row")
    ordered = own_first(corrections, 1).reshape(nodes, n, share)
    summed = row_sum([ordered[:, d] for d in range(n)])
    squares = jnp.sum(inv_two * inv_two, axis=1)
    live_share = lax.dynamic_slice_in_dim(live, me * share, share, 1)
    square_share = lax.dynamic_slice_in_dim(squares, me * share, share, 1)
    var_two = live_share * (square_share - summed)
    return (var_one, var_two, jnp.stack(block_j), jnp.stack(block_r))


def solution(mesh):
    return jax.shard_map(
        body,
        mesh=mesh,
        in_specs=(
            P(("groups", "row"), None),
            P(("groups", "col"), "row", None),
            P(("groups", "col"), None, None),
            P(("groups", "col"), "row", None),
            P(("groups", "col"), "row", None),
            P(("groups", "col"), None, None),
            P(("groups", "col")),
            P(("groups", "col")),
            P(("groups", "col"), "row"),
            P(("groups", "col"), "row"),
        ),
        out_specs=(
            P(("groups", "col"), "row"),
            P(("groups", "col"), "row"),
            P(("groups", "col"), "row", None),
            P(("groups", "col"), "row", None),
        ),
        check_vma=False,
    )
```

profile of v0, /device:TPU:0, one launch (start us, length us, event | category | flops | bytes accessed | tf_op | source)
XLA Modules:
  0.0 283.1 jit_solution(10372713962109828890)
XLA Ops:
  12.9 4.8 %fusion.59 = f32[512,1024]{1,0:T(8,128)} fusion(f32[1,512,1024]{2,1,0:T(8,128)S(1)} %copy-done, f32[1024,256]{1,0:T(8,128)S(1)} %get-tuple-element.17, f32[1024,256]{1,0:T(8,128)S(1)} %get-tuple-element.18, f32[1024,256]{1,0:T(8,128)S(1)} %get-tuple-element.16, f32[1024,256]{1,0:T(8,128)S(1)} %get-tuple-element.11), kind=kOutput, calls=%fused_computation.65 | convolution fusion | flops 3224371200 | bytes 8388608 | tf_op jit(solution)/shard_map/dot_general | solution.py:11
  18.0 3.0 %collective-permute-start.1 = (f32[512,1024]{1,0:T(8,128)}, f32[512,1024]{1,0:T(8,128)}, u32[]{:S(2)}, u32[]{:S(2)}) collective-permute-start(f32[512,1024]{1,0:T(8,128)} %fusion.59), channel_id=1, source_target_pairs={{0,8},{4,12},{8,0},{12,4},{1,9},{5,13},{9,1},{13,5},{2,10},{6,14},... | collective-permute-start | bytes 6291464 | tf_op jit(solution)/shard_map/ppermute | solution.py:22
  23.5 43.5 %collective-permute-done.1 = f32[512,1024]{1,0:T(8,128)} collective-permute-done((f32[512,1024]{1,0:T(8,128)}, f32[512,1024]{1,0:T(8,128)}, u32[]{:S(2)}, u32[]{:S(2)}) %collective-permute-start.1) | collective-permute-done | bytes 2097184 | tf_op jit(solution)/shard_map/ppermute | solution.py:22
  71.7 5.4 %fusion.38 = f32[256,1024]{1,0:T(8,128)} fusion(f32[1024,256]{1,0:T(8,128)} %copy-done.16, f32[1024,256]{1,0:T(8,128)} %copy-done.18, f32[1024,256]{1,0:T(8,128)} %copy-done.19, f32[1024,256]{1,0:T(8,128)} %copy-done.17), kind=kOutput, calls=%fused_computation.41 | convolution fusion | flops 1613758464 | bytes 5242880 | tf_op jit(solution)/shard_map/dot_general | solution.py:15
  77.4 4.4 %constant_dynamic-slice_fusion.13 = (f32[512,512]{1,0:T(8,128)}, f32[512,512]{1,0:T(8,128)}, f32[512,512]{1,0:T(8,128)}, f32[512,512]{1,0:T(8,128)}) fusion(f32[512,2048]{1,0:T(8,128)} %param.10, s32[]{:T(128)S(6)} %select_n.52, s32[]{:T(128)S(6)} %select_n.53, s32[]{:T(128)S(6)} %select_n.55, s32[]{:T(128)S(6)} %select_n.54), kind=kLoop, calls=%fused_computation.151 | loop fusion | bytes 8388624 | tf_op jit(solution)/shard_map/dynamic_slice | solution.py:30
  83.9 11.8 %collective-permute-done.7 = f32[256,1024]{1,0:T(8,128)} collective-permute-done((f32[256,1024]{1,0:T(8,128)}, f32[256,1024]{1,0:T(8,128)}, u32[]{:S(2)}, u32[]{:S(2)}) %collective-permute-start.7) | collective-permute-done | bytes 1048608 | tf_op jit(solution)/shard_map/ppermute | solution.py:22
  95.6 2.9 %fusion.156 = (f32[512,256]{1,0:T(8,128)}, f32[512,256]{1,0:T(8,128)}, f32[512,256]{1,0:T(8,128)}, f32[512,256]{1,0:T(8,128)}) fusion(f32[512,1024]{1,0:T(8,128)} %collective-permute-done), kind=kLoop, calls=%fused_computation.179 | loop fusion | bytes 4194304 | tf_op jit(solution)/shard_map/slice | solution.py:61
  98.5 3.1 %fusion.157 = (f32[512,512]{1,0:T(8,128)}, f32[512,512]{1,0:T(8,128)}) fusion(f32[512,1024]{1,0:T(8,128)} %collective-permute-done.1), kind=kLoop, calls=%fused_computation.180 | loop fusion | bytes 4194304 | tf_op jit(solution)/shard_map/slice | solution.py:61
  101.6 2.9 %fusion.158 = (f32[512,256]{1,0:T(8,128)}, f32[512,256]{1,0:T(8,128)}, f32[512,256]{1,0:T(8,128)}, f32[512,256]{1,0:T(8,128)}) fusion(f32[512,1024]{1,0:T(8,128)} %collective-permute-done.2), kind=kLoop, calls=%fused_computation.181 | loop fusion | bytes 4194304 | tf_op jit(solution)/shard_map/slice | solution.py:61
  104.5 17.1 %multiply_reduce_fusion.1 = f32[1024]{0:T(1024)S(1)} fusion(f32[512,1024]{1,0:T(8,128)} %fusion.59, f32[512,256]{1,0:T(8,128)} %get-tuple-element.30, f32[512,256]{1,0:T(8,128)} %get-tuple-element.31, f32[512,256]{1,0:T(8,128)} %get-tuple-element.32, f32[512,256]{1,0:T(8,128)} %get-tuple-element.29, f32[512,512]{1,0:T(8,128)} %get-tuple-element.28, ...), kind=kOutput, calls=%fused_computation.54 | convolution fusion | flops 6467615744 | bytes 12587008 | tf_op jit(solution)/shard_map/dot_general | solution.py:11
  126.6 4.4 %pad_maximum_fusion.2 = f32[1024,1024]{1,0:T(8,128)} fusion(f32[256,1024]{1,0:T(8,128)} %collective-permute-done.8, f32[256,1024]{1,0:T(8,128)} %collective-permute-done.7, f32[256,1024]{1,0:T(8,128)} %collective-permute-done.6, f32[256,512]{1,0:T(8,128)S(1)} %fusion.98, f32[256,512]{1,0:T(8,128)S(1)} %fusion.102), kind=kLoop, calls=%fused_computation.24 | loop fusion | flops 4194304 | bytes 8388608 | tf_op jit(solution)/shard_map/concatenate | solution.py:101
  131.6 38.7 %all-gather.5.cloned.1.call-done = f32[2048,1024]{1,0:T(8,128)} async-done(((f32[512,1024]{1,0:T(8,128)}), f32[2048,1024]{1,0:T(8,128)}) %all-gather.5.cloned.1.call-update) | async-done | bytes 8388624 | tf_op jit(solution)/shard_map/all_gather | solution.py:85
  170.3 5.3 %fusion.69 = f32[512,512]{1,0:T(8,128)} fusion(f32[512,512]{1,0:T(8,128)} %fusion.92, f32[1024,1024]{1,0:T(8,128)} %pad_maximum_fusion.2, f32[4,512,1024]{2,1,0:T(8,128)} %bitcast.104, s32[]{:T(128)S(6)} %select_n.58), kind=kOutput, calls=%fused_computation.67 | convolution fusion | flops 1610874880 | bytes 6291460 | tf_op jit(solution)/shard_map/dot_general | solution.py:11
  179.2 2.5 fusion.95
  181.7 4.2 %fusion.64 = f32[512,512]{1,0:T(8,128)S(1)} fusion(f32[512,512]{1,0:T(8,128)S(1)} %fusion.95, f32[1024,1024]{1,0:T(8,128)} %pad_maximum_fusion.2, f32[4,512,1024]{2,1,0:T(8,128)} %bitcast.105, s32[]{:T(128)S(6)} %select_n.57), kind=kOutput, calls=%fused_computation.66 | convolution fusion | flops 1610874880 | bytes 6291460 | tf_op jit(solution)/shard_map/dot_general | solution.py:11
  186.6 15.3 %collective-permute-done.16 = f32[512,512]{1,0:T(8,128)} collective-permute-done((f32[512,512]{1,0:T(8,128)}, f32[512,512]{1,0:T(8,128)}, u32[]{:S(2)}, u32[]{:S(2)}) %collective-permute-start.16) | collective-permute-done | bytes 1048608 | tf_op jit(solution)/shard_map/ppermute | solution.py:22
  202.4 21.0 %collective-permute-done.10 = f32[512,512]{1,0:T(8,128)S(1)} collective-permute-done((f32[512,512]{1,0:T(8,128)S(1)}, f32[512,512]{1,0:T(8,128)S(1)}, u32[]{:S(2)}, u32[]{:S(2)}) %collective-permute-start.10) | collective-permute-done | bytes 1048608 | tf_op jit(solution)/shard_map/ppermute | solution.py:22
  223.4 5.1 %multiply_reduce_fusion.2 = (f32[512]{0:T(512)S(1)}, f32[512,512]{1,0:T(8,128)S(1)}) fusion(f32[512,512]{1,0:T(8,128)S(1)} %copy-done.6, f32[512,512]{1,0:T(8,128)S(1)} %collective-permute-done.17, f32[512,512]{1,0:T(8,128)} %collective-permute-done.16, f32[512,512]{1,0:T(8,128)S(1)} %collective-permute-done.15, f32[512,512]{1,0:T(8,128)} %fusion.69, ...), kind=kOutput, calls=%fused_computation.88 | convolution fusion | flops 3228302848 | bytes 10487808 | tf_op jit(solution)/shard_map/dot_general | solution.py:11
  231.9 5.1 %multiply_reduce_fusion.3 = (f32[512]{0:T(512)S(1)}, f32[512,512]{1,0:T(8,128)S(1)}) fusion(f32[512,512]{1,0:T(8,128)S(1)} %fusion.95, f32[512,512]{1,0:T(8,128)} %collective-permute-done.11, f32[512,512]{1,0:T(8,128)S(1)} %collective-permute-done.10, f32[512,512]{1,0:T(8,128)S(1)} %collective-permute-done.9, f32[512,512]{1,0:T(8,128)S(1)} %fusion.64, ...), kind=kOutput, calls=%fused_computation.93 | convolution fusion | flops 3228302848 | bytes 10487808 | tf_op jit(solution)/shard_map/dot_general | solution.py:11
  246.0 4.9 %all-gather.7.cloned.1.call-done = f32[1024,1024]{1,0:T(8,128)} async-done(((f32[256,1024]{1,0:T(8,128)}), f32[1024,1024]{1,0:T(8,128)}) %all-gather.7.cloned.1.call-update) | async-done | bytes 4194320 | tf_op jit(solution)/shard_map/all_gather | solution.py:88
  250.9 5.6 %collective-permute-done.20 = f32[256,512]{1,0:T(8,128)} collective-permute-done((f32[256,512]{1,0:T(8,128)}, f32[256,512]{1,0:T(8,128)}, u32[]{:S(2)}, u32[]{:S(2)}) %collective-permute-start.20) | collective-permute-done | bytes 524320 | tf_op jit(solution)/shard_map/ppermute | solution.py:22
  256.5 3.4 %multiply_reduce_fusion.5 = (f32[512]{0:T(512)S(1)}, f32[256,512]{1,0:T(8,128)S(1)}) fusion(f32[256,512]{1,0:T(8,128)S(1)} %fusion.98, f32[256,512]{1,0:T(8,128)} %collective-permute-done.20, f32[256,512]{1,0:T(8,128)} %collective-permute-done.18, f32[1024,512]{1,0:T(8,128)} %copy-done.4, f32[1024,1024]{1,0:T(8,128)} %pad_maximum_fusion.2, ...), kind=kOutput, calls=%fused_computation.115 | convolution fusion | flops 806092288 | bytes 5769220 | tf_op jit(solution)/shard_map/dot_general | solution.py:11
  260.0 6.8 %collective-permute-done.14 = f32[256,512]{1,0:T(8,128)} collective-permute-done((f32[256,512]{1,0:T(8,128)}, f32[256,512]{1,0:T(8,128)}, u32[]{:S(2)}, u32[]{:S(2)}) %collective-permute-start.14) | collective-permute-done | bytes 524320 | tf_op jit(solution)/shard_map/ppermute | solution.py:22
  266.8 3.1 %multiply_reduce_fusion.6 = (f32[512]{0:T(512)S(1)}, f32[256,512]{1,0:T(8,128)S(1)}) fusion(f32[256,512]{1,0:T(8,128)S(1)} %fusion.102, f32[256,512]{1,0:T(8,128)} %collective-permute-done.14, f32[256,512]{1,0:T(8,128)} %collective-permute-done.12, f32[1024,512]{1,0:T(8,128)} %copy-done.5, f32[1024,1024]{1,0:T(8,128)S(1)} %copy-done.2, ...), kind=kOutput, calls=%fused_computation.118 | convolution fusion | flops 806092288 | bytes 5769220 | tf_op jit(solution)/shard_map/dot_general | solution.py:11
  (138 shorter events, 40.3 us)
Async XLA Ops:
  7.2 163.1 %all-gather.5.cloned.1.call-start = ((), (), s32[]{:S(2)}) async-start(), calls=%async_computation | async-start | bytes 10485760 | tf_op jit(solution)/shard_map/all_gather | solution.py:85
  17.8 233.1 %all-gather.7.cloned.1.call-start = ((), (), s32[]{:S(2)}) async-start(), calls=%async_computation.1 | async-start | bytes 5242880 | tf_op jit(solution)/shard_map/all_gather | solution.py:88
  18.0 49.0 %collective-permute-start.1 = (f32[512,1024]{1,0:T(8,128)}, f32[512,1024]{1,0:T(8,128)}, u32[]{:S(2)}, u32[]{:S(2)}) collective-permute-start(f32[512,1024]{1,0:T(8,128)} %fusion.59), channel_id=1, source_target_pairs={{0,8},{4,12},{8,0},{12,4},{1,9},{5,13},{9,1},{13,5},{2,10},{6,14},... | collective-permute-start | bytes 6291464 | tf_op jit(solution)/shard_map/ppermute | solution.py:22
  21.0 74.6 %collective-permute-start = (f32[512,1024]{1,0:T(8,128)}, f32[512,1024]{1,0:T(8,128)}, u32[]{:S(2)}, u32[]{:S(2)}) collective-permute-start(f32[512,1024]{1,0:T(8,128)} %fusion.59), channel_id=1, source_target_pairs={{0,4},{4,0},{8,12},{12,8},{1,5},{5,1},{9,13},{13,9},{2,6},{6,2},{1... | collective-permute-start | bytes 6291464 | tf_op jit(solution)/shard_map/ppermute | solution.py:22
  67.0 34.6 %collective-permute-start.2 = (f32[512,1024]{1,0:T(8,128)}, f32[512,1024]{1,0:T(8,128)}, u32[]{:S(2)}, u32[]{:S(2)}) collective-permute-start(f32[512,1024]{1,0:T(8,128)} %collective-permute-done.1), channel_id=1, source_target_pairs={{0,4},{4,0},{8,12},{12,8},{1,5},{5,1},{9,13},{13,9},{2,6},{6,2},{1... | collective-permute-start | bytes 6291464 | tf_op jit(solution)/shard_map/ppermute | solution.py:22
  69.7 25.9 %collective-permute-start.7 = (f32[256,1024]{1,0:T(8,128)}, f32[256,1024]{1,0:T(8,128)}, u32[]{:S(2)}, u32[]{:S(2)}) collective-permute-start(f32[256,1024]{1,0:T(8,128)} %pad_maximum_fusion.8), channel_id=1, source_target_pairs={{0,8},{4,12},{8,0},{12,4},{1,9},{5,13},{9,1},{13,5},{2,10},{6,14},... | collective-permute-start | bytes 3145736 | tf_op jit(solution)/shard_map/ppermute | solution.py:22
  71.5 55.1 %collective-permute-start.6 = (f32[256,1024]{1,0:T(8,128)}, f32[256,1024]{1,0:T(8,128)}, u32[]{:S(2)}, u32[]{:S(2)}) collective-permute-start(f32[256,1024]{1,0:T(8,128)} %pad_maximum_fusion.8), channel_id=1, source_target_pairs={{0,4},{4,0},{8,12},{12,8},{1,5},{5,1},{9,13},{13,9},{2,6},{6,2},{1... | collective-permute-start | bytes 3145736 | tf_op jit(solution)/shard_map/ppermute | solution.py:22
  95.6 31.0 %collective-permute-start.8 = (f32[256,1024]{1,0:T(8,128)}, f32[256,1024]{1,0:T(8,128)}, u32[]{:S(2)}, u32[]{:S(2)}) collective-permute-start(f32[256,1024]{1,0:T(8,128)} %collective-permute-done.7), channel_id=1, source_target_pairs={{0,4},{4,0},{8,12},{12,8},{1,5},{5,1},{9,13},{13,9},{2,6},{6,2},{1... | collective-permute-start | bytes 3145736 | tf_op jit(solution)/shard_map/ppermute | solution.py:22
  121.6 3.2 %collective-permute-start.4 = (f32[256]{0:T(256)S(1)}, f32[256]{0:T(256)S(1)}, u32[]{:S(2)}, u32[]{:S(2)}) collective-permute-start(f32[256]{0:T(256)S(1)} %get-tuple-element.42), channel_id=1, source_target_pairs={{0,4},{4,0},{8,12},{12,8},{1,5},{5,1},{9,13},{13,9},{2,6},{6,2},{1... | collective-permute-start | bytes 3080 | tf_op jit(solution)/shard_map/ppermute | solution.py:22
  124.7 6.3 %collective-permute-start.3 = (f32[256]{0:T(256)S(1)}, f32[256]{0:T(256)S(1)}, u32[]{:S(2)}, u32[]{:S(2)}) collective-permute-start(f32[256]{0:T(256)S(1)} %get-tuple-element.41), channel_id=1, source_target_pairs={{0,4},{4,0},{8,12},{12,8},{1,5},{5,1},{9,13},{13,9},{2,6},{6,2},{1... | collective-permute-start | bytes 3080 | tf_op jit(solution)/shard_map/ppermute | solution.py:22
  124.8 6.2 %collective-permute-start.5 = (f32[256]{0:T(256)S(1)}, f32[256]{0:T(256)S(1)}, u32[]{:S(2)}, u32[]{:S(2)}) collective-permute-start(f32[256]{0:T(256)S(1)} %slice_add_fusion.4), channel_id=1, source_target_pairs={{0,8},{4,12},{8,0},{12,4},{1,9},{5,13},{9,1},{13,5},{2,10},{6,14},... | collective-permute-start | bytes 3080 | tf_op jit(solution)/shard_map/ppermute | solution.py:22
  175.6 26.3 %collective-permute-start.16 = (f32[512,512]{1,0:T(8,128)}, f32[512,512]{1,0:T(8,128)}, u32[]{:S(2)}, u32[]{:S(2)}) collective-permute-start(f32[512,512]{1,0:T(8,128)} %fusion.69), channel_id=1, source_target_pairs={{0,8},{4,12},{8,0},{12,4},{1,9},{5,13},{9,1},{13,5},{2,10},{6,14},... | collective-permute-start | bytes 3145736 | tf_op jit(solution)/shard_map/ppermute | solution.py:22
  186.0 37.4 %collective-permute-start.10 = (f32[512,512]{1,0:T(8,128)S(1)}, f32[512,512]{1,0:T(8,128)S(1)}, u32[]{:S(2)}, u32[]{:S(2)}) collective-permute-start(f32[512,512]{1,0:T(8,128)S(1)} %fusion.64), channel_id=1, source_target_pairs={{0,8},{4,12},{8,0},{12,4},{1,9},{5,13},{9,1},{13,5},{2,10},{6,14},... | collective-permute-start | bytes 3145736 | tf_op jit(solution)/shard_map/ppermute | solution.py:22
  186.6 36.8 %collective-permute-start.15 = (f32[512,512]{1,0:T(8,128)}, f32[512,512]{1,0:T(8,128)S(1)}, u32[]{:S(2)}, u32[]{:S(2)}) collective-permute-start(f32[512,512]{1,0:T(8,128)} %fusion.69), channel_id=1, source_target_pairs={{0,4},{4,0},{8,12},{12,8},{1,5},{5,1},{9,13},{13,9},{2,6},{6,2},{1... | collective-permute-start | bytes 3145736 | tf_op jit(solution)/shard_map/ppermute | solution.py:22
  201.9 21.5 %collective-permute-start.17 = (f32[512,512]{1,0:T(8,128)}, f32[512,512]{1,0:T(8,128)S(1)}, u32[]{:S(2)}, u32[]{:S(2)}) collective-permute-start(f32[512,512]{1,0:T(8,128)} %collective-permute-done.16), channel_id=1, source_target_pairs={{0,4},{4,0},{8,12},{12,8},{1,5},{5,1},{9,13},{13,9},{2,6},{6,2},{1... | collective-permute-start | bytes 3145736 | tf_op jit(solution)/shard_map/ppermute | solution.py:22
  201.9 30.0 %collective-permute-start.9 = (f32[512,512]{1,0:T(8,128)S(1)}, f32[512,512]{1,0:T(8,128)S(1)}, u32[]{:S(2)}, u32[]{:S(2)}) collective-permute-start(f32[512,512]{1,0:T(8,128)S(1)} %fusion.64), channel_id=1, source_target_pairs={{0,4},{4,0},{8,12},{12,8},{1,5},{5,1},{9,13},{13,9},{2,6},{6,2},{1... | collective-permute-start | bytes 3145736 | tf_op jit(solution)/shard_map/ppermute | solution.py:22
  223.4 8.6 %collective-permute-start.11 = (f32[512,512]{1,0:T(8,128)S(1)}, f32[512,512]{1,0:T(8,128)}, u32[]{:S(2)}, u32[]{:S(2)}) collective-permute-start(f32[512,512]{1,0:T(8,128)S(1)} %collective-permute-done.10), channel_id=1, source_target_pairs={{0,4},{4,0},{8,12},{12,8},{1,5},{5,1},{9,13},{13,9},{2,6},{6,2},{1... | collective-permute-start | bytes 3145736 | tf_op jit(solution)/shard_map/ppermute | solution.py:22
  231.4 9.1 %collective-permute-start.19 = (f32[256,512]{1,0:T(8,128)S(1)}, f32[256,512]{1,0:T(8,128)S(1)}, u32[]{:S(2)}, u32[]{:S(2)}) collective-permute-start(f32[256,512]{1,0:T(8,128)S(1)} %get-tuple-element.22), channel_id=1, source_target_pairs={{0,4},{4,0},{8,12},{12,8},{1,5},{5,1},{9,13},{13,9},{2,6},{6,2},{1... | collective-permute-start | bytes 1572872 | tf_op jit(solution)/shard_map/ppermute | solution.py:22
  240.0 10.9 %collective-permute-start.18 = (f32[256,512]{1,0:T(8,128)}, f32[256,512]{1,0:T(8,128)}, u32[]{:S(2)}, u32[]{:S(2)}) collective-permute-start(f32[256,512]{1,0:T(8,128)} %get-tuple-element.21), channel_id=1, source_target_pairs={{0,4},{4,0},{8,12},{12,8},{1,5},{5,1},{9,13},{13,9},{2,6},{6,2},{1... | collective-permute-start | bytes 1572872 | tf_op jit(solution)/shard_map/ppermute | solution.py:22
  241.4 15.1 %collective-permute-start.20 = (f32[256,512]{1,0:T(8,128)}, f32[256,512]{1,0:T(8,128)}, u32[]{:S(2)}, u32[]{:S(2)}) collective-permute-start(f32[256,512]{1,0:T(8,128)} %slice_add_fusion), channel_id=1, source_target_pairs={{0,8},{4,12},{8,0},{12,4},{1,9},{5,13},{9,1},{13,5},{2,10},{6,14},... | collective-permute-start | bytes 1572872 | tf_op jit(solution)/shard_map/ppermute | solution.py:22
  242.9 17.1 %collective-permute-start.12 = (f32[256,512]{1,0:T(8,128)}, f32[256,512]{1,0:T(8,128)}, u32[]{:S(2)}, u32[]{:S(2)}) collective-permute-start(f32[256,512]{1,0:T(8,128)} %get-tuple-element.19), channel_id=1, source_target_pairs={{0,4},{4,0},{8,12},{12,8},{1,5},{5,1},{9,13},{13,9},{2,6},{6,2},{1... | collective-permute-start | bytes 1572872 | tf_op jit(solution)/shard_map/ppermute | solution.py:22
  244.9 21.8 %collective-permute-start.14 = (f32[256,512]{1,0:T(8,128)}, f32[256,512]{1,0:T(8,128)}, u32[]{:S(2)}, u32[]{:S(2)}) collective-permute-start(f32[256,512]{1,0:T(8,128)} %slice_add_fusion.2), channel_id=1, source_target_pairs={{0,8},{4,12},{8,0},{12,4},{1,9},{5,13},{9,1},{13,5},{2,10},{6,14},... | collective-permute-start | bytes 1572872 | tf_op jit(solution)/shard_map/ppermute | solution.py:22
  271.6 3.0 %collective-permute-start.21 = (f32[2,128]{1,0:T(2,128)S(1)}, f32[2,128]{1,0:T(2,128)S(1)}, u32[]{:S(2)}, u32[]{:S(2)}) collective-permute-start(f32[2,128]{1,0:T(2,128)S(1)} %get-tuple-element.33), channel_id=1, source_target_pairs={{0,4},{4,0},{8,12},{12,8},{1,5},{5,1},{9,13},{13,9},{2,6},{6,2},{1... | collective-permute-start | bytes 3080 | tf_op jit(solution)/shard_map/ppermute | solution.py:22
  272.1 3.6 %collective-permute-start.23 = (f32[2,128]{1,0:T(2,128)S(1)}, f32[2,128]{1,0:T(2,128)S(1)}, u32[]{:S(2)}, u32[]{:S(2)}) collective-permute-start(f32[2,128]{1,0:T(2,128)S(1)} %fusion.146), channel_id=1, source_target_pairs={{0,8},{4,12},{8,0},{12,4},{1,9},{5,13},{9,1},{13,5},{2,10},{6,14},... | collective-permute-start | bytes 3080 | tf_op jit(solution)/shard_map/ppermute | solution.py:22
  (28 other events, 493.9 us)
Sparse Core Ops, SparseCore 0:
  17.9 152.3 all-gather.4
  171.8 78.9 all-gather.6
where the time goes:
time: 284 us; the launch traced here: 283 us
  waiting for transfers between devices  149 us (52%)
  matrix products  65.5 us (23%)
  local copies, waits for them, and re-layouts  20.7 us (7%)
  between operations  18.4 us (6%)
  starting transfers between devices  15.6 us (5%)
  other arithmetic  14 us (5%)
    ppermute x24, waiting for transfers between devices, swap(): return lax.ppermute(block, 'row', [(i, i ^ bit) for i in range(n)])  105 us
    dot_general x12, matrix products, product(): jnp.dot(left, right, precision=PRECISION, preferred_element_type=jnp.floa...  56.4 us
    all_gather x1, waiting for transfers between devices, body(): all_factors = lax.all_gather(factor, 'col', axis=0)  38.7 us
    ppermute x24, starting transfers between devices, swap(): return lax.ppermute(block, 'row', [(i, i ^ bit) for i in range(n)])  15.4 us
    dot_general x3, matrix products, crossed(): lax.dot_general(left, right, (((0,), (0,)), ((), ())), precision=PRECISIO...  9.15 us
    slice x3, local copies, waits for them, and re-layouts, reordered(): block[:, (d ^ e) * share:((d ^ e) + 1) * share]  8.82 us
    dynamic_slice x2, local copies, waits for them, and re-layouts, own_first(): lax.dynamic_slice_in_dim(array, (me ^ d) * share, share, axis)  6.9 us
  transfers between devices with their start and end apart: 26, of which 9 were waited for; matrix products, arithmetic and copies ran while one was open for 30% of the time, Pallas kernels for 0%

commit v1 on v0

--- a/solution.py
+++ b/solution.py
@@ -1,6 +1,8 @@
 import jax
 import jax.numpy as jnp
 from jax import lax
+from jax.experimental import pallas as pl
+from jax.experimental.pallas import tpu as pltpu
 from jax.sharding import PartitionSpec as P
 
 TILE = 64
@@ -62,7 +64,7 @@
     )
 
 
-def body(
+def general_body(
     zroot,
     panel_one,
     inv_one,
@@ -147,9 +149,516 @@
     return (var_one, var_two, jnp.stack(block_j), jnp.stack(block_r))
 
 
+PIECE = 32
+RING = 8
+AHEAD = 2
+STEP = 128
+
+
+def mm(left, right):
+    return jnp.dot(left, right, precision=PRECISION, preferred_element_type=jnp.float32)
+
+
+def mm_t(left, right):
+    return lax.dot_general(
+        left, right, (((0,), (0,)), ((), ())), precision=PRECISION, preferred_element_type=jnp.float32
+    )
+
+
+def exchange_kernel(
+    picks,
+    own,
+    near_j,
+    near_r,
+    root,
+    z_j,
+    z_r,
+    var_a,
+    var_b,
+    held,
+    staged,
+    full_j,
+    chosen,
+    reduced,
+    across,
+    beside,
+    part_in,
+    part_y,
+    vec_a,
+    vec_b,
+    line_send,
+    line_recv,
+    j_send,
+    j_recv,
+    g_send,
+    g_recv,
+    r_send,
+    r_recv,
+    u_send,
+    u_recv,
+    a_send,
+    a_recv,
+    b_send,
+    b_recv,
+):
+    rows = root.shape[0]
+    width = own.shape[1]
+    node = near_j.shape[0]
+    nodes, _, two = z_r.shape
+    chunks = own.shape[0] // PIECE
+    steps = rows // STEP
+    per = STEP // PIECE
+    half = width // 2
+
+    z = lax.axis_index("col")
+    r = lax.axis_index("row")
+    core = r % 2
+    side = r // 2
+    twin = r + 1 - 2 * core
+    over = (r + 2) % 4
+    diag = (twin + 2) % 4
+    inner = jnp.logical_or(z == 1, z == 2)
+    outer = jnp.logical_not(inner)
+
+    def remote(src, dst, send, recv, device):
+        return pltpu.make_async_remote_copy(
+            src_ref=src,
+            dst_ref=dst,
+            send_sem=send,
+            recv_sem=recv,
+            device_id=device,
+            device_id_type=pl.DeviceIdType.MESH,
+        )
+
+    def at_row(index):
+        return (lax.axis_index("groups"), index, z)
+
+    def at_col(index):
+        return (lax.axis_index("groups"), r, index)
+
+    barrier = pltpu.get_barrier_semaphore()
+
+    def greet(device):
+        pl.semaphore_signal(barrier, inc=1, device_id=device, device_id_type=pl.DeviceIdType.MESH)
+
+    for peer in (twin, over, diag):
+        greet(at_row(peer))
+
+    @pl.when(outer)
+    def _():
+        greet(at_col(1 + z // 3))
+        pl.semaphore_wait(barrier, 4)
+
+    @pl.when(inner)
+    def _():
+        greet(at_col(3 - z))
+        greet(at_col(((z - 1) * 3) % 4))
+        pl.semaphore_wait(barrier, 5)
+
+    def piece(t):
+        return pl.ds(pl.multiple_of(t * PIECE, PIECE), PIECE)
+
+    def line(stream, t):
+        at = piece(t)
+        if stream == 0:
+            src, dst, device = own.at[at], held.at[2, at], at_col(1 + z // 3)
+        elif stream == 1:
+            src, dst, device = own.at[at], held.at[0, at], at_col(3 - z)
+        elif stream == 2:
+            src, dst, device = held.at[2, at], held.at[1, at], at_col(3 - z)
+        else:
+            src = staged.at[stream - 3, piece(t % RING)]
+            dst, device = held.at[stream - 3, at], at_col(((z - 1) * 3) % 4)
+        return remote(src, dst, line_send.at[stream, t], line_recv.at[stream, t], device)
+
+    def to_middle(t):
+        line(1, t).start()
+        line(0, t).wait_recv()
+        line(2, t).start()
+
+    def chunk(t):
+        @pl.when(inner)
+        def _():
+            @pl.when(t + AHEAD < chunks)
+            def _():
+                to_middle(t + AHEAD)
+
+            line(1, t).wait_recv()
+            line(2, t).wait_recv()
+            at = piece(t)
+            for m in range(nodes):
+                pick = picks[nodes + m]
+
+                @pl.when(t >= RING)
+                def _():
+                    line(3 + m, t - RING).wait_send()
+
+                staged[m, piece(t % RING), :] = jnp.where(
+                    pick == 0, own[at, :], jnp.where(pick == 1, held[0, at, :], held[1, at, :])
+                )
+                line(3 + m, t).start()
+
+        @pl.when(outer)
+        def _():
+            line(3, t).wait_recv()
+            line(4, t).wait_recv()
+
+    def j_copy(k):
+        mine = pl.ds(pl.multiple_of(r * node, node), node)
+        theirs = pl.ds(pl.multiple_of(over * node, node), node)
+        if k == 2:
+            return remote(full_j.at[theirs], full_j.at[theirs], j_send.at[2], j_recv.at[2], at_row(twin))
+        return remote(near_j, full_j.at[mine], j_send.at[k], j_recv.at[k], at_row(over if k == 0 else twin))
+
+    def g_copy(k):
+        at = pl.ds(pl.multiple_of(core * rows, rows), rows)
+        top = pl.ds(0, rows)
+        if k == 0:
+            columns = pl.ds(pl.multiple_of((1 - side) * half, half), half)
+            return remote(own.at[top, columns], across.at[at], g_send.at[0], g_recv.at[0], at_row(over))
+        if k == 1:
+            columns = pl.ds(pl.multiple_of((1 - core) * half, half), half)
+            return remote(own.at[top, columns], beside, g_send.at[1], g_recv.at[1], at_row(twin))
+        return remote(across.at[at], across.at[at], g_send.at[2], g_recv.at[2], at_row(twin))
+
+    def r_copy(k, step):
+        who = over if k == 2 else r
+        at = pl.ds(pl.multiple_of(who * rows + step * STEP, STEP), STEP)
+        return remote(
+            reduced.at[at],
+            reduced.at[at],
+            r_send.at[k, step],
+            r_recv.at[k, step],
+            at_row(over if k == 0 else twin),
+        )
+
+    @pl.when(outer)
+    def _():
+        def go(t, carry):
+            line(0, t).start()
+            return carry
+
+        lax.fori_loop(0, chunks, go, 0)
+
+    for k in (0, 1):
+        j_copy(k).start()
+
+    @pl.when(inner)
+    def _():
+        def go(t, carry):
+            to_middle(t)
+            return carry
+
+        lax.fori_loop(0, AHEAD, go, 0)
+
+    for k in (0, 1):
+        g_copy(k).start()
+
+    mine_j = pl.ds(pl.multiple_of(r * node, node), node)
+    full_j[mine_j, :] = near_j[...]
+    for m in range(nodes):
+        z_r[m] = jnp.zeros_like(z_r[m])
+
+    def pick_rows(m, at):
+        pick = picks[m]
+        first = jnp.where(pick == 0, own[at, :], held[0, at, :])
+        second = jnp.where(pick == 2, held[1, at, :], held[2, at, :])
+        return jnp.where(pick < 2, first, second)
+
+    def reduce_step(step):
+        at = pl.ds(pl.multiple_of(step * STEP, STEP), STEP)
+        to = pl.ds(pl.multiple_of(r * rows + step * STEP, STEP), STEP)
+        for m in range(nodes):
+            block = pick_rows(m, at)
+            chosen[m, at, :] = block
+            columns = slice(m * two, (m + 1) * two)
+            reduced[to, columns] = near_r[at, columns] - mm(block, full_j[:, columns])
+        r_copy(0, step).start()
+        r_copy(1, step).start()
+
+    def gather_step(step):
+        r_copy(0, step).wait_recv()
+        r_copy(2, step).start()
+
+    def root_step(step):
+        r_copy(1, step).wait_recv()
+        r_copy(2, step).wait_recv()
+        places = [pl.ds(pl.multiple_of(d * rows + step * STEP, STEP), STEP) for d in range(4)]
+        left = jnp.concatenate([root[:, place] for place in places], 1)
+        for m in range(nodes):
+            columns = slice(m * two, (m + 1) * two)
+            right = jnp.concatenate([reduced[place, columns] for place in places], 0)
+            z_r[m] -= mm(left, right)
+
+    def to_tile(vec):
+        return jnp.concatenate([vec[:, i * 128 : (i + 1) * 128] for i in range(vec.shape[1] // 128)], 0)
+
+    def to_peers(tile, send, recv):
+        return [
+            remote(tile.at[0], tile.at[1 + k], send.at[k], recv.at[k], at_row(peer))
+            for k, peer in enumerate((twin, over, diag))
+        ]
+
+    def level_one():
+        def colsum(at, where):
+            return jnp.sum(at * where, axis=0, keepdims=True)
+
+        mine = pl.ds(pl.multiple_of(r * rows, rows), rows)
+        theirs = pl.ds(pl.multiple_of(twin * rows, rows), rows)
+        far = pl.ds(pl.multiple_of((1 - side) * 2 * rows, 2 * rows), 2 * rows)
+        sums = []
+        for h in range(2):
+            columns = slice(h * half, (h + 1) * half)
+            block = own[0:rows, columns]
+            sums.append(colsum(block, mm(root[:, mine], block)))
+        g_copy(1).wait_recv()
+        pair = mm(root[:, theirs], beside[...])
+        lift = pl.ds(pl.multiple_of(core * half, half), half)
+        pair = 2.0 * colsum(own[0:rows, lift], pair)
+        g_copy(2).wait_recv()
+        cross = mm(root[:, far], across[...])
+        lift = pl.ds(pl.multiple_of(side * half, half), half)
+        cross = 2.0 * colsum(own[0:rows, lift], cross)
+        for h in range(2):
+            sums[h] = sums[h] + jnp.where(core == h, pair, 0.0) + jnp.where(side == h, cross, 0.0)
+        vec_a[0] = to_tile(jnp.concatenate(sums, 1))
+
+    def walk(base):
+        def go(s, carry):
+            chunk(base + s)
+            return carry
+
+        return go
+
+    lax.fori_loop(0, per, walk(0), 0)
+    j_copy(0).wait_recv()
+    j_copy(2).start()
+    j_copy(1).wait_recv()
+    j_copy(2).wait_recv()
+    reduce_step(0)
+    g_copy(0).wait_recv()
+    g_copy(2).start()
+
+    def macro(step, carry):
+        lax.fori_loop(0, per - 1, walk(step * per), 0)
+        gather_step(step - 1)
+        chunk(step * per + per - 1)
+        root_step(step - 1)
+        reduce_step(step)
+        return carry
+
+    lax.fori_loop(1, 2, macro, 0)
+    level_one()
+    for copy in to_peers(vec_a, a_send, a_recv):
+        copy.start()
+    lax.fori_loop(2, steps, macro, 0)
+
+    def node_step(step):
+        at = pl.ds(rows + step * STEP, STEP)
+        for m in range(nodes):
+            z_j[m, step * STEP : (step + 1) * STEP, :] = mm(
+                pick_rows(m, at), full_j[:, m * two : (m + 1) * two]
+            )
+
+    base = steps * per
+    lax.fori_loop(base, base + per - 1, walk(0), 0)
+    gather_step(steps - 1)
+    root_step(steps - 1)
+
+    parts = full_j.shape[0] // node
+    part_out = across
+    part_own = beside
+
+    def upper(m, dest):
+        columns = pl.ds(pl.multiple_of(dest * node, node), node)
+        return mm_t(chosen[m, :, columns], z_r[m])
+
+    def u_copy(k):
+        at = pl.ds(0, 2 * node)
+        if k < 2:
+            return remote(part_out.at[pl.ds(k * 2 * node, 2 * node)], part_in.at[k], u_send.at[k], u_recv.at[k], at_row(twin))
+        return remote(part_own.at[pl.ds((k - 2) * node, node)], part_y.at[k - 2], u_send.at[k], u_recv.at[k], at_row(over))
+
+    for copy in (g_copy(0), g_copy(1), g_copy(2)):
+        copy.wait_send()
+    for m in range(nodes):
+        part_out[m * 2 * node : m * 2 * node + node, :] = upper(m, diag)
+        part_out[m * 2 * node + node : (m + 1) * 2 * node, :] = upper(m, twin)
+        u_copy(m).start()
+    chunk(base + per - 1)
+    for m in range(nodes):
+        far = upper(m, over)
+        u_copy(m).wait_recv()
+        part_own[m * node : (m + 1) * node, :] = far + part_in[m, 0:node, :]
+        u_copy(2 + m).start()
+    node_step(0)
+    for m in range(nodes):
+        part_in[m, node : 2 * node, :] = part_in[m, node : 2 * node, :] + upper(m, r)
+    for copy in to_peers(vec_a, a_send, a_recv):
+        copy.wait()
+    var_a[...] = vec_a[0] + vec_a[1] + vec_a[2] + vec_a[3]
+    sums_r = [
+        jnp.sum(near_r[:, m * two : (m + 1) * two] * z_r[m], axis=0, keepdims=True) for m in range(nodes)
+    ]
+    lax.fori_loop(base + per, base + 2 * per, walk(0), 0)
+    node_step(1)
+    for m in range(nodes):
+        u_copy(2 + m).wait_recv()
+        z_j[m] = -(z_j[m] + part_in[m, node : 2 * node, :] + part_y[m])
+        sums_r[m] = sums_r[m] + jnp.sum(near_j[:, m * two : (m + 1) * two] * z_j[m], axis=0, keepdims=True)
+    vec_b[0] = to_tile(jnp.concatenate(sums_r, 1))
+    for copy in to_peers(vec_b, b_send, b_recv):
+        copy.start()
+
+    @pl.when(outer)
+    def _():
+        def go(t, carry):
+            line(0, t).wait_send()
+            return carry
+
+        lax.fori_loop(0, chunks, go, 0)
+
+    @pl.when(inner)
+    def _():
+        def go(t, carry):
+            line(1, t).wait_send()
+            line(2, t).wait_send()
+            return carry
+
+        lax.fori_loop(0, chunks, go, 0)
+
+        def last(t, carry):
+            line(3, t).wait_send()
+            line(4, t).wait_send()
+            return carry
+
+        lax.fori_loop(chunks - RING, chunks, last, 0)
+
+    for k in range(3):
+        j_copy(k).wait_send()
+
+    def sent(step, carry):
+        for k in range(3):
+            r_copy(k, step).wait_send()
+        return carry
+
+    lax.fori_loop(0, steps, sent, 0)
+    for k in range(4):
+        u_copy(k).wait_send()
+    for copy in to_peers(vec_b, b_send, b_recv):
+        copy.wait()
+    var_b[...] = vec_b[0] + vec_b[1] + vec_b[2] + vec_b[3]
+
+
+def line_body(
+    zroot,
+    panel_one,
+    inv_one,
+    panel_two_j,
+    panel_two_r,
+    inv_two,
+    parents,
+    widths,
+    pattern_j,
+    pattern_r,
+):
+    n = lax.axis_size("row")
+    width = inv_one.shape[1]
+    node = width // n
+    nodes, two = inv_two.shape[:2]
+    rows = zroot.shape[0]
+    me = lax.axis_index("row")
+    z = lax.axis_index("col")
+
+    low = z < 2
+    beyond = lax.ppermute(parents, "col", [(0, 1), (3, 2)])
+    place = jnp.where(low, z, 3 - z)
+    ours = jnp.where(low, parents, 3 - parents)
+    theirs = jnp.where(low, beyond, 3 - beyond)
+    slot = jnp.arange(1, nodes + 1, dtype=jnp.int32)
+    ours = jnp.where(place == 1, (ours + 3) % 4, jnp.where(ours == 0, 0, slot))
+    picks = jnp.concatenate([ours, jnp.maximum(theirs - 1, 0)]).astype(jnp.int32)
+
+    inverse = inv_one[0]
+    mine = lax.dynamic_slice_in_dim(inverse, me * node, node, 1)
+    own = jnp.concatenate([product(panel_one[0], inverse), crossed(mine, inverse)], 0)
+
+    live = (jnp.arange(two)[None, :] < widths[:, None]).astype(jnp.float32)
+    mask_j = jnp.repeat(pattern_j.astype(jnp.float32), TILE, axis=1)
+    mask_r = jnp.repeat(pattern_r.astype(jnp.float32), TILE, axis=1)
+    factor_j = []
+    factor_r = []
+    for i in range(nodes):
+        masked_j = panel_two_j[i] * mask_j[i][:, None] * live[i][None, :]
+        masked_r = panel_two_r[i] * mask_r[i][:, None] * live[i][None, :]
+        factor_j.append(product(masked_j, inv_two[i]))
+        factor_r.append(product(masked_r, inv_two[i]))
+    near_j = jnp.concatenate(factor_j, 1)
+    near_r = jnp.concatenate(factor_r, 1)
+
+    chunks = own.shape[0] // PIECE
+    steps = rows // STEP
+    f32 = jnp.float32
+    vmem = pl.BlockSpec(memory_space=pltpu.VMEM)
+    dma = pltpu.SemaphoreType.DMA
+    z_j, z_r, sums_a, sums_b = pl.pallas_call(
+        exchange_kernel,
+        out_shape=(
+            jax.ShapeDtypeStruct((nodes, node, two), f32),
+            jax.ShapeDtypeStruct((nodes, rows, two), f32),
+            jax.ShapeDtypeStruct((width // 128, 128), f32),
+            jax.ShapeDtypeStruct((nodes * two // 128, 128), f32),
+        ),
+        in_specs=[pl.BlockSpec(memory_space=pltpu.SMEM)] + [vmem] * 4,
+        out_specs=(vmem,) * 4,
+        scratch_shapes=[
+            pltpu.VMEM((3,) + own.shape, f32),
+            pltpu.VMEM((nodes, RING * PIECE, width), f32),
+            pltpu.VMEM((width, nodes * two), f32),
+            pltpu.VMEM((nodes, rows, width), f32),
+            pltpu.VMEM((4 * rows, nodes * two), f32),
+            pltpu.VMEM((2 * rows, width // 2), f32),
+            pltpu.VMEM((rows, width // 2), f32),
+            pltpu.VMEM((nodes, 2 * node, two), f32),
+            pltpu.VMEM((nodes, node, two), f32),
+            pltpu.VMEM((4, width // 128, 128), f32),
+            pltpu.VMEM((4, nodes * two // 128, 128), f32),
+            dma((5, chunks)),
+            dma((5, chunks)),
+            dma((3,)),
+            dma((3,)),
+            dma((3,)),
+            dma((3,)),
+            dma((3, steps)),
+            dma((3, steps)),
+            dma((4,)),
+            dma((4,)),
+            dma((3,)),
+            dma((3,)),
+            dma((3,)),
+            dma((3,)),
+        ],
+        compiler_params=pltpu.CompilerParams(
+            collective_id=0, has_side_effects=True, vmem_limit_bytes=61 * 1024 * 1024
+        ),
+    )(picks, own, near_j, near_r, zroot)
+
+    share_one = width // n
+    squares = jnp.sum(mine**2, axis=0)
+    corr_one = lax.dynamic_slice_in_dim(sums_a.reshape(width), me * share_one, share_one, 0)
+    var_one = (squares + corr_one)[None, :]
+    share = two // n
+    squares_two = lax.dynamic_slice_in_dim(jnp.sum(inv_two * inv_two, axis=1), me * share, share, 1)
+    corr_two = lax.dynamic_slice_in_dim(sums_b.reshape(nodes, two), me * share, share, 1)
+    live_share = lax.dynamic_slice_in_dim(live, me * share, share, 1)
+    var_two = live_share * (squares_two - corr_two)
+    return (var_one, var_two, z_j, z_r)
+
+
 def solution(mesh):
+    fits = mesh.shape["row"] == 4 and mesh.shape["col"] == 4
     return jax.shard_map(
-        body,
+        line_body if fits else general_body,
         mesh=mesh,
         in_specs=(
             P(("groups", "row"), None),

time: 284 us -> 219 us (0.77)
  Pallas kernels: 0 us -> 175 us
  waiting for transfers between devices: 149 us -> 0.01 us
  matrix products: 65.5 us -> 19.8 us
  between operations: 18.4 us -> 0.79 us
  local copies, waits for them, and re-layouts: 20.7 us -> 5.23 us
  starting transfers between devices: 15.6 us -> 5.06 us
    pallas_call x0 -> x1, Pallas kernels: none -> 175 us  [line_body(): pl.pallas_call(exchange_kernel, out_shape=(jax.ShapeDtypeStruct((nodes, n...]
    ppermute x24 -> x1, waiting for transfers between devices: 105 us -> 0.01 us  [line_body(): beyond = lax.ppermute(parents, 'col', [(0, 1), (3, 2)])]
    all_gather x2 -> x0, waiting for transfers between devices: 43.6 us -> none  [the longest x1 38.7 us: body(): all_factors = lax.all_gather(factor, 'col', axis=0)]
    dot_general x12 -> x5, matrix products: 56.4 us -> 14.4 us  [product(): jnp.dot(left, right, precision=PRECISION, preferred_element_type=jnp.floa...]
    slice x10 -> x3, local copies, waits for them, and re-layouts: 11.5 us -> 0.02 us  [the longest x2 0.01 us: line_body(): masked_j = panel_two_j[i] * mask_j[i][:, None] * live[i][None, :]]
    ppermute x24 -> x1, starting transfers between devices: 15.4 us -> 5.06 us  [line_body(): beyond = lax.ppermute(parents, 'col', [(0, 1), (3, 2)])]
    dynamic_slice x2 -> x0, local copies, waits for them, and re-layouts: 6.9 us -> none  [own_first(): lax.dynamic_slice_in_dim(array, (me ^ d) * share, share, axis)]
    dot_general x3 -> x1, matrix products: 9.15 us -> 5.43 us  [crossed(): lax.dot_general(left, right, (((0,), (0,)), ((), ())), precision=PRECISIO...]
  transfers between devices with their start and end apart: 26 -> 1, of which waited for: 9 -> 0; matrix products, arithmetic and copies ran while one was open for 30% -> 14% of each run, Pallas kernels for 0% -> 0%
where the time goes in v1:
time: 219 us; the launch traced here: 218 us
  Pallas kernels  175 us (80%)
  matrix products  19.8 us (9%)
  other arithmetic  12.6 us (6%)
  local copies, waits for them, and re-layouts  5.23 us (2%)
  starting transfers between devices  5.06 us (2%)
    pallas_call x1, Pallas kernels, line_body(): pl.pallas_call(exchange_kernel, out_shape=(jax.ShapeDtypeStruct((nodes, n...  175 us
    dot_general x5, matrix products, product(): jnp.dot(left, right, precision=PRECISION, preferred_element_type=jnp.floa...  14.4 us
    dot_general x1, matrix products, crossed(): lax.dot_general(left, right, (((0,), (0,)), ((), ())), precision=PRECISIO...  5.43 us
    ppermute x1, starting transfers between devices, line_body(): beyond = lax.ppermute(parents, 'col', [(0, 1), (3, 2)])  5.06 us
  transfers between devices with their start and end apart: 1, of which 0 were waited for; matrix products, arithmetic and copies ran while one was open for 14% of the time, Pallas kernels for 0%

profile of v1, /device:TPU:0, one launch (start us, length us, event | category | flops | bytes accessed | tf_op | source)
XLA Modules:
  0.0 218.4 jit_solution(17631523187489775594)
XLA Ops:
  0.6 5.1 %collective-permute-start = (s32[2]{0:T(128)}, s32[2]{0:T(128)S(1)}, u32[]{:S(2)}, u32[]{:S(2)}) collective-permute-start(s32[2]{0:T(128)} %param.16), channel_id=1, source_target_pairs={{0,1},{3,2},{4,5},{7,6},{8,9},{11,10},{12,13},{15,14},{16,17},{19,... | collective-permute-start | bytes 32 | tf_op jit(solution)/shard_map/ppermute | solution.py:574
  5.7 5.4 %fusion = f32[256,1024]{1,0:T(8,128)} fusion(f32[1,1024,1024]{2,1,0:T(8,128)} %param.12, s32[]{:T(128)S(6)} %select_n.41), kind=kOutput, calls=%fused_computation | convolution fusion | flops 1610612736 | bytes 6291460 | tf_op jit(solution)/shard_map/dot_general | solution.py:17
  11.2 1.4 fusion.16
  12.6 7.0 %fusion.2 = f32[512,1024]{1,0:T(8,128)} fusion(f32[1,1024,1024]{2,1,0:T(8,128)} %param.12, f32[1,512,1024]{2,1,0:T(8,128)S(1)} %copy-done), kind=kOutput, calls=%fused_computation.2 | convolution fusion | flops 3221225472 | bytes 8388608 | tf_op jit(solution)/shard_map/dot_general | solution.py:13
  19.8 0.1 broadcast_in_dim.32
  20.0 0.1 broadcast_in_dim.30
  20.1 0.1 broadcast_in_dim.28
  20.3 0.1 broadcast_in_dim.26
  20.4 1.9 multiply_reduce_fusion
  22.3 0.3 copy-done.1
  22.6 2.4 %fusion.5 = f32[512,512]{1,0:T(8,128)S(1)} fusion(f32[2,512,512]{2,1,0:T(8,128)} %param.14, f32[2,512,512]{2,1,0:T(8,128)S(1)} %copy-done.1, f32[512]{0:T(512)S(1)} %bitcast.50, f32[512]{0:T(512)S(1)} %broadcast_in_dim.32), kind=kOutput, calls=%fused_computation.9 | convolution fusion | flops 805830656 | bytes 3149824 | tf_op jit(solution)/shard_map/dot_general | solution.py:13
  25.0 2.1 fusion.7
  27.1 1.4 fusion.10
  28.6 1.4 fusion.13
  30.0 4.0 %pad_maximum_fusion.own = f32[768,1024]{1,0:T(8,128)} fusion(f32[256,1024]{1,0:T(8,128)} %fusion, f32[512,1024]{1,0:T(8,128)} %fusion.2), kind=kLoop, calls=%fused_computation.4 | loop fusion | flops 786432 | bytes 6291456 | tf_op jit(solution)/shard_map/concatenate | solution.py:584
  34.0 1.5 pad_maximum_fusion.1.near_r
  35.6 1.0 pad_maximum_fusion.2.near_j
  36.6 0.6 pad_add_fusion.picks
  37.2 174.9 %shard_map.129 = (f32[2,256,512]{2,1,0:T(8,128)}, f32[2,512,512]{2,1,0:T(8,128)}, f32[8,128]{1,0:T(8,128)}, f32[8,128]{1,0:T(8,128)}) custom-call(s32[4]{0:T(128)} %pad_add_fusion.picks, f32[768,1024]{1,0:T(8,128)} %pad_maximum_fusion.own, f32[256,1024]{1,0:T(8,128)} %pad_maximum_fusion.2.near_j, f32[512,1024]{1,0:T(8,128)} %pad_maximum_fusion.1.near_r, ...), custom_call_target="tpu_custom_call" | custom-call | tf_op jit(solution)/shard_map/pallas_call | solution.py:604
  212.1 0.7 reshape.95
  212.8 1.5 dynamic-slice_add_fusion
  214.2 0.6 subtract_multiply_fusion
  214.8 2.3 %copy.20 = f32[2,256,512]{2,1,0:T(8,128)} copy(f32[2,256,512]{2,1,0:T(8,128)} %get-tuple-element.24) | data formatting | bytes 2097152
  217.1 1.3 copy.21
  (36 shorter events, 0.5 us)
Async XLA Ops:
  0.6 11.9 %copy-start = (f32[1,512,1024]{2,1,0:T(8,128)S(1)}, f32[1,512,1024]{2,1,0:T(8,128)}, u32[]{:S(2)}) copy-start(f32[1,512,1024]{2,1,0:T(8,128)} %param.11) | copy-start | bytes 6291460
  0.6 36.0 %collective-permute-start = (s32[2]{0:T(128)}, s32[2]{0:T(128)S(1)}, u32[]{:S(2)}, u32[]{:S(2)}) collective-permute-start(s32[2]{0:T(128)} %param.16), channel_id=1, source_target_pairs={{0,1},{3,2},{4,5},{7,6},{8,9},{11,10},{12,13},{15,14},{16,17},{19,... | collective-permute-start | bytes 32 | tf_op jit(solution)/shard_map/ppermute | solution.py:574
  5.7 6.8 %copy-start.11 = (s32[2]{0:T(128)S(1)}, s32[2]{0:T(128)}, u32[]{:S(2)}) copy-start(s32[2]{0:T(128)} %param.16) | copy-start | bytes 28
  12.6 7.1 %copy-start.10 = (s32[2]{0:T(128)S(1)}, s32[2]{0:T(128)}, u32[]{:S(2)}) copy-start(s32[2]{0:T(128)} %param.17) | copy-start | bytes 28
  12.6 7.1 %copy-start.8 = (s32[2,8]{1,0:T(2,128)S(1)}, s32[2,8]{1,0:T(2,128)}, u32[]{:S(2)}) copy-start(s32[2,8]{1,0:T(2,128)} %param.19) | copy-start | bytes 196
  12.6 7.5 %copy-start.9 = (s32[2,4]{1,0:T(2,128)S(1)}, s32[2,4]{1,0:T(2,128)}, u32[]{:S(2)}) copy-start(s32[2,4]{1,0:T(2,128)} %param.18) | copy-start | bytes 100
  20.4 2.2 %copy-start.1 = (f32[2,512,512]{2,1,0:T(8,128)S(1)}, f32[2,512,512]{2,1,0:T(8,128)}, u32[]{:S(2)}) copy-start(f32[2,512,512]{2,1,0:T(8,128)} %param.15) | copy-start | bytes 6291460
  22.3 2.7 %copy-start.3 = (f32[2,512,512]{2,1,0:T(8,128)S(1)}, f32[2,512,512]{2,1,0:T(8,128)}, u32[]{:S(2)}) copy-start(f32[2,512,512]{2,1,0:T(8,128)} %param.14) | copy-start | bytes 6291460
  25.0 2.1 copy-start.7
  30.0 4.0 %copy-start.2 = (f32[512,512]{1,0:T(8,128)S(1)}, f32[512,512]{1,0:T(8,128)}, u32[]{:S(2)}) copy-start(f32[512,512]{1,0:T(8,128)} %fusion.7) | copy-start | bytes 3145732
  34.0 1.5 copy-start.5
  34.0 1.5 copy-start.6
  212.8 4.3 %copy-start.4 = (f32[2,512,512]{2,1,0:T(8,128)S(1)}, f32[2,512,512]{2,1,0:T(8,128)}, u32[]{:S(2)}) copy-start(f32[2,512,512]{2,1,0:T(8,128)} %get-tuple-element.25) | copy-start | bytes 6291460

commit v2 on v1

--- a/solution.py
+++ b/solution.py
@@ -151,7 +151,7 @@
 
 PIECE = 32
 RING = 8
-AHEAD = 2
+AHEAD = 4
 STEP = 128
 
 
@@ -165,16 +165,25 @@
     )
 
 
-def exchange_kernel(
-    picks,
+def line_kernel(
+    parents,
+    widths,
+    tiles_j,
+    tiles_r,
+    zroot,
+    panel_one,
+    inv_one,
+    panel_j,
+    panel_r,
+    inv_two,
+    var_one,
+    var_two,
+    z_j,
+    z_r,
+    root,
     own,
     near_j,
     near_r,
-    root,
-    z_j,
-    z_r,
-    var_a,
-    var_b,
     held,
     staged,
     full_j,
@@ -184,8 +193,12 @@
     beside,
     part_in,
     part_y,
+    note,
     vec_a,
     vec_b,
+    loads,
+    note_send,
+    note_recv,
     line_send,
     line_recv,
     j_send,
@@ -236,6 +249,31 @@
     def at_col(index):
         return (lax.axis_index("groups"), r, index)
 
+    def span(index, size):
+        return pl.ds(pl.multiple_of(index * size, size), size)
+
+    def child(m):
+        return pl.ds(m * two, two)
+
+    def load(k):
+        if k == 0:
+            return pltpu.make_async_copy(panel_one.at[0], own.at[pl.ds(0, rows)], loads.at[0])
+        if k < 3:
+            h = k - 1
+            return pltpu.make_async_copy(inv_one.at[0, pl.ds(h * half, half)], chosen.at[h], loads.at[k])
+        if k < 5:
+            m = k - 3
+            return pltpu.make_async_copy(panel_j.at[m], near_j.at[:, child(m)], loads.at[k])
+        if k == 5:
+            return pltpu.make_async_copy(inv_two, part_in, loads.at[5])
+        if k < 8:
+            m = k - 6
+            return pltpu.make_async_copy(panel_r.at[m], near_r.at[:, child(m)], loads.at[k])
+        return pltpu.make_async_copy(zroot, root, loads.at[8])
+
+    for k in range(9):
+        load(k).start()
+
     barrier = pltpu.get_barrier_semaphore()
 
     def greet(device):
@@ -247,19 +285,39 @@
     @pl.when(outer)
     def _():
         greet(at_col(1 + z // 3))
-        pl.semaphore_wait(barrier, 4)
 
     @pl.when(inner)
     def _():
         greet(at_col(3 - z))
         greet(at_col(((z - 1) * 3) % 4))
+
+    low = z < 2
+    place = jnp.where(low, z, 3 - z)
+    kin = [jnp.where(low, parents[m], 3 - parents[m]) for m in range(nodes)]
+    picks = [
+        jnp.where(place == 1, (kin[m] + 3) % 4, jnp.where(kin[m] == 0, 0, 1 + m)) for m in range(nodes)
+    ]
+    note[0] = jnp.zeros(note.shape[1:], jnp.int32)
+    for m in range(nodes):
+        note[0, m : m + 1, :] = jnp.full((1, width), kin[m], jnp.int32)
+
+    @pl.when(outer)
+    def _():
+        pl.semaphore_wait(barrier, 4)
+
+    @pl.when(inner)
+    def _():
         pl.semaphore_wait(barrier, 5)
 
-    def piece(t):
-        return pl.ds(pl.multiple_of(t * PIECE, PIECE), PIECE)
+    def note_copy():
+        return remote(note.at[0], note.at[1], note_send, note_recv, at_col(1 + z // 3))
+
+    @pl.when(outer)
+    def _():
+        note_copy().start()
 
     def line(stream, t):
-        at = piece(t)
+        at = span(t, PIECE)
         if stream == 0:
             src, dst, device = own.at[at], held.at[2, at], at_col(1 + z // 3)
         elif stream == 1:
@@ -267,12 +325,20 @@
         elif stream == 2:
             src, dst, device = held.at[2, at], held.at[1, at], at_col(3 - z)
         else:
-            src = staged.at[stream - 3, piece(t % RING)]
+            src = staged.at[stream - 3, span(t % RING, PIECE)]
             dst, device = held.at[stream - 3, at], at_col(((z - 1) * 3) % 4)
         return remote(src, dst, line_send.at[stream, t], line_recv.at[stream, t], device)
 
-    def to_middle(t):
-        line(1, t).start()
+    def to_inner(first, last):
+        @pl.when(outer)
+        def _():
+            def go(t, carry):
+                line(0, t).start()
+                return carry
+
+            lax.fori_loop(first, last, go, 0)
+
+    def forward(t):
         line(0, t).wait_recv()
         line(2, t).start()
 
@@ -281,20 +347,21 @@
         def _():
             @pl.when(t + AHEAD < chunks)
             def _():
-                to_middle(t + AHEAD)
+                line(1, t + AHEAD).start()
+                forward(t + AHEAD)
 
             line(1, t).wait_recv()
             line(2, t).wait_recv()
-            at = piece(t)
+            at = span(t, PIECE)
             for m in range(nodes):
-                pick = picks[nodes + m]
+                pick = note[1, m : m + 1, :]
 
                 @pl.when(t >= RING)
                 def _():
                     line(3 + m, t - RING).wait_send()
 
-                staged[m, piece(t % RING), :] = jnp.where(
-                    pick == 0, own[at, :], jnp.where(pick == 1, held[0, at, :], held[1, at, :])
+                staged[m, span(t % RING, PIECE), :] = jnp.where(
+                    pick < 2, own[at, :], jnp.where(pick == 2, held[0, at, :], held[1, at, :])
                 )
                 line(3 + m, t).start()
 
@@ -304,20 +371,20 @@
             line(4, t).wait_recv()
 
     def j_copy(k):
-        mine = pl.ds(pl.multiple_of(r * node, node), node)
-        theirs = pl.ds(pl.multiple_of(over * node, node), node)
+        mine = span(r, node)
+        theirs = span(over, node)
         if k == 2:
             return remote(full_j.at[theirs], full_j.at[theirs], j_send.at[2], j_recv.at[2], at_row(twin))
         return remote(near_j, full_j.at[mine], j_send.at[k], j_recv.at[k], at_row(over if k == 0 else twin))
 
     def g_copy(k):
-        at = pl.ds(pl.multiple_of(core * rows, rows), rows)
+        at = span(core, rows)
         top = pl.ds(0, rows)
         if k == 0:
-            columns = pl.ds(pl.multiple_of((1 - side) * half, half), half)
+            columns = span(1 - side, half)
             return remote(own.at[top, columns], across.at[at], g_send.at[0], g_recv.at[0], at_row(over))
         if k == 1:
-            columns = pl.ds(pl.multiple_of((1 - core) * half, half), half)
+            columns = span(1 - core, half)
             return remote(own.at[top, columns], beside, g_send.at[1], g_recv.at[1], at_row(twin))
         return remote(across.at[at], across.at[at], g_send.at[2], g_recv.at[2], at_row(twin))
 
@@ -332,33 +399,6 @@
             at_row(over if k == 0 else twin),
         )
 
-    @pl.when(outer)
-    def _():
-        def go(t, carry):
-            line(0, t).start()
-            return carry
-
-        lax.fori_loop(0, chunks, go, 0)
-
-    for k in (0, 1):
-        j_copy(k).start()
-
-    @pl.when(inner)
-    def _():
-        def go(t, carry):
-            to_middle(t)
-            return carry
-
-        lax.fori_loop(0, AHEAD, go, 0)
-
-    for k in (0, 1):
-        g_copy(k).start()
-
-    mine_j = pl.ds(pl.multiple_of(r * node, node), node)
-    full_j[mine_j, :] = near_j[...]
-    for m in range(nodes):
-        z_r[m] = jnp.zeros_like(z_r[m])
-
     def pick_rows(m, at):
         pick = picks[m]
         first = jnp.where(pick == 0, own[at, :], held[0, at, :])
@@ -366,13 +406,12 @@
         return jnp.where(pick < 2, first, second)
 
     def reduce_step(step):
-        at = pl.ds(pl.multiple_of(step * STEP, STEP), STEP)
+        at = span(step, STEP)
         to = pl.ds(pl.multiple_of(r * rows + step * STEP, STEP), STEP)
         for m in range(nodes):
             block = pick_rows(m, at)
             chosen[m, at, :] = block
-            columns = slice(m * two, (m + 1) * two)
-            reduced[to, columns] = near_r[at, columns] - mm(block, full_j[:, columns])
+            reduced[to, child(m)] = near_r[at, child(m)] - mm(block, full_j[:, child(m)])
         r_copy(0, step).start()
         r_copy(1, step).start()
 
@@ -380,18 +419,24 @@
         r_copy(0, step).wait_recv()
         r_copy(2, step).start()
 
-    def root_step(step):
+    def root_wait(step):
         r_copy(1, step).wait_recv()
         r_copy(2, step).wait_recv()
+
+    def root_step(step, m):
         places = [pl.ds(pl.multiple_of(d * rows + step * STEP, STEP), STEP) for d in range(4)]
-        left = jnp.concatenate([root[:, place] for place in places], 1)
-        for m in range(nodes):
-            columns = slice(m * two, (m + 1) * two)
-            right = jnp.concatenate([reduced[place, columns] for place in places], 0)
-            z_r[m] -= mm(left, right)
+        left = jnp.concatenate([root[:, at] for at in places], 1)
+        right = jnp.concatenate([reduced[at, child(m)] for at in places], 0)
+        z_r[m] -= mm(left, right)
 
     def to_tile(vec):
         return jnp.concatenate([vec[:, i * 128 : (i + 1) * 128] for i in range(vec.shape[1] // 128)], 0)
+
+    def shared(pieces):
+        total = jnp.zeros_like(pieces[0])
+        for d, one in enumerate(pieces):
+            total = total + jnp.where(r == d, one, 0.0)
+        return total
 
     def to_peers(tile, send, recv):
         return [
@@ -399,119 +444,213 @@
             for k, peer in enumerate((twin, over, diag))
         ]
 
-    def level_one():
-        def colsum(at, where):
-            return jnp.sum(at * where, axis=0, keepdims=True)
-
-        mine = pl.ds(pl.multiple_of(r * rows, rows), rows)
-        theirs = pl.ds(pl.multiple_of(twin * rows, rows), rows)
-        far = pl.ds(pl.multiple_of((1 - side) * 2 * rows, 2 * rows), 2 * rows)
-        sums = []
-        for h in range(2):
-            columns = slice(h * half, (h + 1) * half)
-            block = own[0:rows, columns]
-            sums.append(colsum(block, mm(root[:, mine], block)))
-        g_copy(1).wait_recv()
-        pair = mm(root[:, theirs], beside[...])
-        lift = pl.ds(pl.multiple_of(core * half, half), half)
-        pair = 2.0 * colsum(own[0:rows, lift], pair)
-        g_copy(2).wait_recv()
-        cross = mm(root[:, far], across[...])
-        lift = pl.ds(pl.multiple_of(side * half, half), half)
-        cross = 2.0 * colsum(own[0:rows, lift], cross)
-        for h in range(2):
-            sums[h] = sums[h] + jnp.where(core == h, pair, 0.0) + jnp.where(side == h, cross, 0.0)
-        vec_a[0] = to_tile(jnp.concatenate(sums, 1))
-
-    def walk(base):
-        def go(s, carry):
-            chunk(base + s)
-            return carry
-
-        return go
-
-    lax.fori_loop(0, per, walk(0), 0)
+    def colsum(left, right):
+        return jnp.sum(left * right, axis=0, keepdims=True)
+
+    def factor(first, size):
+        at = pl.ds(first, size)
+        own[at, :] = mm(own[at, 0:half], chosen[0]) + mm(own[at, half:width], chosen[1])
+
+    for k in range(3):
+        load(k).wait()
+    factor(0, STEP)
+    to_inner(0, per)
+
+    @pl.when(inner)
+    def _():
+        line(1, 0).start()
+        line(1, 1).start()
+
+    factor(STEP, rows - STEP)
+    to_inner(per, steps * per)
+
+    @pl.when(inner)
+    def _():
+        forward(0)
+        line(1, 2).start()
+        forward(1)
+        line(1, 3).start()
+
+    def masked(panel, tiles, at, m, first, count):
+        column = lax.broadcasted_iota(jnp.int32, (1, two), 1)
+        live = (column < widths[m]).astype(jnp.float32)
+        blocks = [
+            panel[pl.ds(at + i * TILE, TILE), child(m)] * (live * tiles[m, first + i].astype(jnp.float32))
+            for i in range(count)
+        ]
+        return jnp.concatenate(blocks, 0)
+
+    for k in range(3, 6):
+        load(k).wait()
+    for m in range(nodes):
+        near_j[:, child(m)] = mm(masked(near_j, tiles_j, 0, m, 0, node // TILE), part_in[m])
+    for k in (0, 1):
+        j_copy(k).start()
+    for k in (0, 1):
+        g_copy(k).start()
+
+    @pl.when(inner)
+    def _():
+        forward(2)
+        forward(3)
+        note_copy().wait_recv()
+
+    full_j[span(r, node), :] = near_j[...]
+    for k in range(6, 8):
+        load(k).wait()
+    for m in range(nodes):
+        near_r[:, child(m)] = mm(masked(near_r, tiles_r, 0, m, 0, rows // TILE), part_in[m])
+        z_r[m] = jnp.zeros_like(z_r[m])
+    chunk(0)
+
+    def gram(k):
+        columns = pl.ds(pl.multiple_of(r * node + k * STEP, STEP), STEP)
+        own[rows + k * STEP : rows + (k + 1) * STEP, :] = mm_t(chosen[0, :, columns], chosen[0]) + mm_t(
+            chosen[1, :, columns], chosen[1]
+        )
+        to_inner((steps + k) * per, (steps + k + 1) * per)
+
+    gram(0)
+    chunk(1)
+    gram(1)
+    chunk(2)
+    squares_one = sum(
+        colsum(chosen[h, :, span(r, node)], chosen[h, :, span(r, node)]) for h in range(2)
+    )
+    squares_two = [colsum(part_in[m], part_in[m]) for m in range(nodes)]
+    chunk(3)
     j_copy(0).wait_recv()
     j_copy(2).start()
     j_copy(1).wait_recv()
     j_copy(2).wait_recv()
     reduce_step(0)
+
+    load(8).wait()
+    sums = []
+
+    def diagonal(h):
+        block = own[0:rows, h * half : (h + 1) * half]
+        sums.append(colsum(block, mm(root[:, span(r, rows)], block)))
+
+    chunk(per)
     g_copy(0).wait_recv()
     g_copy(2).start()
-
-    def macro(step, carry):
-        lax.fori_loop(0, per - 1, walk(step * per), 0)
-        gather_step(step - 1)
-        chunk(step * per + per - 1)
-        root_step(step - 1)
-        reduce_step(step)
-        return carry
-
-    lax.fori_loop(1, 2, macro, 0)
-    level_one()
+    diagonal(0)
+    chunk(per + 1)
+    gather_step(0)
+    diagonal(1)
+    chunk(per + 2)
+    root_wait(0)
+    root_step(0, 0)
+    chunk(per + 3)
+    reduce_step(1)
+
+    g_copy(1).wait_recv()
+    g_copy(2).wait_recv()
+    chunk(2 * per)
+    root_step(0, 1)
+    pair = mm(root[:, span(twin, rows)], beside[...])
+    pair = 2.0 * colsum(own[0:rows, span(core, half)], pair)
+    chunk(2 * per + 1)
+    gather_step(1)
+    cross = mm(root[:, span(1 - side, 2 * rows)], across[...])
+    cross = 2.0 * colsum(own[0:rows, span(side, half)], cross)
+    chunk(2 * per + 2)
+    root_wait(1)
+    root_step(1, 0)
+    chunk(2 * per + 3)
+    reduce_step(2)
+
+    chunk(3 * per)
+    root_step(1, 1)
+    for h in range(2):
+        sums[h] = sums[h] + jnp.where(core == h, pair, 0.0) + jnp.where(side == h, cross, 0.0)
+    vec_a[0] = to_tile(jnp.concatenate(sums, 1))
     for copy in to_peers(vec_a, a_send, a_recv):
         copy.start()
-    lax.fori_loop(2, steps, macro, 0)
+    chunk(3 * per + 1)
+    gather_step(2)
+    chunk(3 * per + 2)
+    root_wait(2)
+    root_step(2, 0)
+    chunk(3 * per + 3)
+    reduce_step(3)
 
     def node_step(step):
         at = pl.ds(rows + step * STEP, STEP)
         for m in range(nodes):
-            z_j[m, step * STEP : (step + 1) * STEP, :] = mm(
-                pick_rows(m, at), full_j[:, m * two : (m + 1) * two]
-            )
-
-    base = steps * per
-    lax.fori_loop(base, base + per - 1, walk(0), 0)
-    gather_step(steps - 1)
-    root_step(steps - 1)
-
-    parts = full_j.shape[0] // node
+            z_j[m, step * STEP : (step + 1) * STEP, :] = mm(pick_rows(m, at), full_j[:, child(m)])
+
     part_out = across
     part_own = beside
 
     def upper(m, dest):
-        columns = pl.ds(pl.multiple_of(dest * node, node), node)
-        return mm_t(chosen[m, :, columns], z_r[m])
+        return mm_t(chosen[m, :, span(dest, node)], z_r[m])
 
     def u_copy(k):
-        at = pl.ds(0, 2 * node)
         if k < 2:
-            return remote(part_out.at[pl.ds(k * 2 * node, 2 * node)], part_in.at[k], u_send.at[k], u_recv.at[k], at_row(twin))
-        return remote(part_own.at[pl.ds((k - 2) * node, node)], part_y.at[k - 2], u_send.at[k], u_recv.at[k], at_row(over))
-
-    for copy in (g_copy(0), g_copy(1), g_copy(2)):
-        copy.wait_send()
-    for m in range(nodes):
+            out = part_out.at[pl.ds(k * 2 * node, 2 * node)]
+            return remote(out, part_in.at[k], u_send.at[k], u_recv.at[k], at_row(twin))
+        out = part_own.at[pl.ds((k - 2) * node, node)]
+        return remote(out, part_y.at[k - 2], u_send.at[k], u_recv.at[k], at_row(over))
+
+    def upper_twin(m):
         part_out[m * 2 * node : m * 2 * node + node, :] = upper(m, diag)
         part_out[m * 2 * node + node : (m + 1) * 2 * node, :] = upper(m, twin)
         u_copy(m).start()
-    chunk(base + per - 1)
-    for m in range(nodes):
+
+    def upper_over(m):
         far = upper(m, over)
         u_copy(m).wait_recv()
         part_own[m * node : (m + 1) * node, :] = far + part_in[m, 0:node, :]
         u_copy(2 + m).start()
+
+    def upper_own(m):
+        part_in[m, node : 2 * node, :] = part_in[m, node : 2 * node, :] + upper(m, r)
+
+    base = steps * per
+    chunk(base)
+    root_step(2, 1)
+    chunk(base + 1)
+    for k in range(3):
+        g_copy(k).wait_send()
+    chunk(base + 2)
+    gather_step(3)
+    root_wait(3)
+    root_step(3, 0)
+    upper_twin(0)
+    root_step(3, 1)
+    upper_twin(1)
+    chunk(base + 3)
+    upper_over(0)
+    upper_over(1)
+    chunk(base + per)
     node_step(0)
+    chunk(base + per + 1)
     for m in range(nodes):
-        part_in[m, node : 2 * node, :] = part_in[m, node : 2 * node, :] + upper(m, r)
+        upper_own(m)
+    chunk(base + per + 2)
     for copy in to_peers(vec_a, a_send, a_recv):
         copy.wait()
-    var_a[...] = vec_a[0] + vec_a[1] + vec_a[2] + vec_a[3]
-    sums_r = [
-        jnp.sum(near_r[:, m * two : (m + 1) * two] * z_r[m], axis=0, keepdims=True) for m in range(nodes)
-    ]
-    lax.fori_loop(base + per, base + 2 * per, walk(0), 0)
+    total = vec_a[0] + vec_a[1] + vec_a[2] + vec_a[3]
+    each = total.shape[0] // 4
+    mine = shared([total[d * each : (d + 1) * each, :] for d in range(4)])
+    var_one[...] = squares_one + jnp.concatenate([mine[i : i + 1, :] for i in range(each)], 1)
+    sums_r = [colsum(near_r[:, child(m)], z_r[m]) for m in range(nodes)]
+    chunk(base + per + 3)
     node_step(1)
     for m in range(nodes):
         u_copy(2 + m).wait_recv()
         z_j[m] = -(z_j[m] + part_in[m, node : 2 * node, :] + part_y[m])
-        sums_r[m] = sums_r[m] + jnp.sum(near_j[:, m * two : (m + 1) * two] * z_j[m], axis=0, keepdims=True)
+        sums_r[m] = sums_r[m] + colsum(near_j[:, child(m)], z_j[m])
     vec_b[0] = to_tile(jnp.concatenate(sums_r, 1))
     for copy in to_peers(vec_b, b_send, b_recv):
         copy.start()
 
     @pl.when(outer)
     def _():
+        note_copy().wait_send()
+
         def go(t, carry):
             line(0, t).wait_send()
             return carry
@@ -547,7 +686,14 @@
         u_copy(k).wait_send()
     for copy in to_peers(vec_b, b_send, b_recv):
         copy.wait()
-    var_b[...] = vec_b[0] + vec_b[1] + vec_b[2] + vec_b[3]
+    total = vec_b[0] + vec_b[1] + vec_b[2] + vec_b[3]
+    share = two // 4
+    column = lax.broadcasted_iota(jnp.int32, (1, share), 1) + r * share
+    for m in range(nodes):
+        mine = shared([total[m * 4 + d : m * 4 + d + 1, :] for d in range(4)])
+        square = shared([squares_two[m][:, d * share : (d + 1) * share] for d in range(4)])
+        live = (column < widths[m]).astype(jnp.float32)
+        var_two[m : m + 1, :] = live * (square - mine)
 
 
 def line_body(
@@ -567,52 +713,29 @@
     node = width // n
     nodes, two = inv_two.shape[:2]
     rows = zroot.shape[0]
-    me = lax.axis_index("row")
-    z = lax.axis_index("col")
-
-    low = z < 2
-    beyond = lax.ppermute(parents, "col", [(0, 1), (3, 2)])
-    place = jnp.where(low, z, 3 - z)
-    ours = jnp.where(low, parents, 3 - parents)
-    theirs = jnp.where(low, beyond, 3 - beyond)
-    slot = jnp.arange(1, nodes + 1, dtype=jnp.int32)
-    ours = jnp.where(place == 1, (ours + 3) % 4, jnp.where(ours == 0, 0, slot))
-    picks = jnp.concatenate([ours, jnp.maximum(theirs - 1, 0)]).astype(jnp.int32)
-
-    inverse = inv_one[0]
-    mine = lax.dynamic_slice_in_dim(inverse, me * node, node, 1)
-    own = jnp.concatenate([product(panel_one[0], inverse), crossed(mine, inverse)], 0)
-
-    live = (jnp.arange(two)[None, :] < widths[:, None]).astype(jnp.float32)
-    mask_j = jnp.repeat(pattern_j.astype(jnp.float32), TILE, axis=1)
-    mask_r = jnp.repeat(pattern_r.astype(jnp.float32), TILE, axis=1)
-    factor_j = []
-    factor_r = []
-    for i in range(nodes):
-        masked_j = panel_two_j[i] * mask_j[i][:, None] * live[i][None, :]
-        masked_r = panel_two_r[i] * mask_r[i][:, None] * live[i][None, :]
-        factor_j.append(product(masked_j, inv_two[i]))
-        factor_r.append(product(masked_r, inv_two[i]))
-    near_j = jnp.concatenate(factor_j, 1)
-    near_r = jnp.concatenate(factor_r, 1)
-
-    chunks = own.shape[0] // PIECE
+    chunks = (rows + node) // PIECE
     steps = rows // STEP
     f32 = jnp.float32
+    smem = pl.BlockSpec(memory_space=pltpu.SMEM)
+    hbm = pl.BlockSpec(memory_space=pl.ANY)
     vmem = pl.BlockSpec(memory_space=pltpu.VMEM)
     dma = pltpu.SemaphoreType.DMA
-    z_j, z_r, sums_a, sums_b = pl.pallas_call(
-        exchange_kernel,
+    return pl.pallas_call(
+        line_kernel,
         out_shape=(
+            jax.ShapeDtypeStruct((1, node), f32),
+            jax.ShapeDtypeStruct((nodes, two // n), f32),
             jax.ShapeDtypeStruct((nodes, node, two), f32),
             jax.ShapeDtypeStruct((nodes, rows, two), f32),
-            jax.ShapeDtypeStruct((width // 128, 128), f32),
-            jax.ShapeDtypeStruct((nodes * two // 128, 128), f32),
         ),
-        in_specs=[pl.BlockSpec(memory_space=pltpu.SMEM)] + [vmem] * 4,
+        in_specs=[smem] * 4 + [hbm] * 6,
         out_specs=(vmem,) * 4,
         scratch_shapes=[
-            pltpu.VMEM((3,) + own.shape, f32),
+            pltpu.VMEM(zroot.shape, f32),
+            pltpu.VMEM((rows + node, width), f32),
+            pltpu.VMEM((node, nodes * two), f32),
+            pltpu.VMEM((rows, nodes * two), f32),
+            pltpu.VMEM((3, rows + node, width), f32),
             pltpu.VMEM((nodes, RING * PIECE, width), f32),
             pltpu.VMEM((width, nodes * two), f32),
             pltpu.VMEM((nodes, rows, width), f32),
@@ -621,8 +744,12 @@
             pltpu.VMEM((rows, width // 2), f32),
             pltpu.VMEM((nodes, 2 * node, two), f32),
             pltpu.VMEM((nodes, node, two), f32),
+            pltpu.VMEM((2, 8, width), jnp.int32),
             pltpu.VMEM((4, width // 128, 128), f32),
             pltpu.VMEM((4, nodes * two // 128, 128), f32),
+            dma((9,)),
+            dma,
+            dma,
             dma((5, chunks)),
             dma((5, chunks)),
             dma((3,)),
@@ -639,20 +766,9 @@
             dma((3,)),
         ],
         compiler_params=pltpu.CompilerParams(
-            collective_id=0, has_side_effects=True, vmem_limit_bytes=61 * 1024 * 1024
+            collective_id=0, has_side_effects=True, vmem_limit_bytes=60 * 1024 * 1024
         ),
-    )(picks, own, near_j, near_r, zroot)
-
-    share_one = width // n
-    squares = jnp.sum(mine**2, axis=0)
-    corr_one = lax.dynamic_slice_in_dim(sums_a.reshape(width), me * share_one, share_one, 0)
-    var_one = (squares + corr_one)[None, :]
-    share = two // n
-    squares_two = lax.dynamic_slice_in_dim(jnp.sum(inv_two * inv_two, axis=1), me * share, share, 1)
-    corr_two = lax.dynamic_slice_in_dim(sums_b.reshape(nodes, two), me * share, share, 1)
-    live_share = lax.dynamic_slice_in_dim(live, me * share, share, 1)
-    var_two = live_share * (squares_two - corr_two)
-    return (var_one, var_two, z_j, z_r)
+    )(parents, widths, pattern_j, pattern_r, zroot, panel_one, inv_one, panel_two_j, panel_two_r, inv_two)
 
 
 def solution(mesh):

time: 219 us -> 193 us (0.88)
  matrix products: 19.8 us -> 0 us
  other arithmetic: 12.6 us -> 0 us
  Pallas kernels: 175 us -> 186 us
  starting transfers between devices: 5.06 us -> 0 us
    dot_general x6 -> x0, matrix products: 19.8 us -> none  [the longest x5 14.4 us: product(): jnp.dot(left, right, precision=PRECISION, preferred_element_type=jnp.floa...]
    pallas_call x1, Pallas kernels: 175 us -> 186 us  [line_body(): pl.pallas_call(line_kernel, out_shape=(jax.ShapeDtypeStruct((1, node), f3...]
    concatenate x4 -> x0, other arithmetic: 7.17 us -> none  [the longest x1 4.04 us: line_body(): jnp.concatenate([product(panel_one[0], inverse), crossed(mine, inverse)], 0)]
    ppermute x1 -> x0, starting transfers between devices: 5.06 us -> none  [line_body(): beyond = lax.ppermute(parents, 'col', [(0, 1), (3, 2)])]
    reduce_sum x2 -> x0, other arithmetic: 3.32 us -> none  [the longest x1 1.94 us: line_body(): jnp.sum(inv_two * inv_two, axis=1)]
    unnamed x26 -> x6, local copies, waits for them, and re-layouts: 3.91 us -> 6.15 us
  transfers between devices with their start and end apart: 1 -> 0, of which waited for: 0 -> 0; matrix products, arithmetic and copies ran while one was open for 14% -> 0% of each run, Pallas kernels for 0% -> 0%
where the time goes in v2:
time: 193 us
  Pallas kernels  186 us (96%)
  local copies, waits for them, and re-layouts  6.15 us (3%)
    pallas_call x1, Pallas kernels, line_body(): pl.pallas_call(line_kernel, out_shape=(jax.ShapeDtypeStruct((1, node), f3...  186 us
    unnamed x6, local copies, waits for them, and re-layouts  6.15 us

profile of v2, /device:TPU:0, one launch (start us, length us, event | category | flops | bytes accessed | tf_op | source)
XLA Modules:
  0.0 192.8 jit_solution(5283261975356277308)
XLA Ops:
  0.6 186.0 %shard_map.129 = (f32[1,256]{1,0:T(1,128)}, f32[2,128]{1,0:T(2,128)}, f32[2,256,512]{2,1,0:T(8,128)}, f32[2,512,512]{2,1,0:T(8,128)}) custom-call(s32[2]{0:T(128)} %parents.1, s32[2]{0:T(128)} %widths.1, s32[2,4]{1,0:T(2,128)} %tiles_j.1, s32[2,8]{1,0:T(2,128)} %tiles_r.1, f32[512,2048]{1,0:T(8,128)} %zroot.1, f32[1,512,1024]{2,1,0:T(8,128)} %panel_one.1, ...), custom_call_target="tpu_custom_call" | custom-call | tf_op jit(solution)/shard_map/pallas_call | solution.py:723
  186.6 0.0 copy-start
  186.6 1.4 copy.18
  188.0 1.2 copy.19
  189.2 2.3 %copy.20 = f32[2,256,512]{2,1,0:T(8,128)} copy(f32[2,256,512]{2,1,0:T(8,128)} %get-tuple-element.10) | data formatting | bytes 2097152
  191.5 0.0 copy-done
  191.5 1.3 copy.21
Async XLA Ops:
  186.6 4.8 %copy-start = (f32[2,512,512]{2,1,0:T(8,128)S(1)}, f32[2,512,512]{2,1,0:T(8,128)}, u32[]{:S(2)}) copy-start(f32[2,512,512]{2,1,0:T(8,128)} %get-tuple-element.11) | copy-start | bytes 6291460
